TPU v7x, 256 devices: a whole 4x4x8 slice. The times are simulated.
256 devices in a mesh: row: 8 (over x, core), col: 32 (over y, z).
Axes of the slice: x: 4, y: 4, z: 8, core: 2. Of those that a mesh axis runs over, the one named last changes fastest.
Arguments:
- activations: bfloat16 [4096, 8192], P('col', 'row'), may hold values from -6 to 6
- out_grads: bfloat16 [4096, 22016], P('row', 'col'), may hold values from -48 to 48
- basis: float32 [8192, 512], P('row'), may hold values from -0.0625 to 0.0625
- row_moment: float32 [512], P('row'), may hold values from 40960 to 409600
- col_moment: float32 [22016], P('col'), may hold values from 4096 to 819200
Outputs:
- weight_update: float32 [8192, 22016], P('row', 'col')
- row_next: float32 [512], P('row')
- col_next: float32 [22016], P('col')
All inputs are finite; a program needn't handle non-finite values.
Results may differ from a plain program's by a relative error of at most 0.0003.
Values may be sent and summed in bfloat16 or wider, within the bound.
A program may use at most 64 MiB of HBM per device.

v0:
```python
import jax
import jax.numpy as jnp
from jax import lax
from jax.sharding import PartitionSpec as P

F = 22016
R = 512


beta_two = 0.8
scale_alpha = 0.25
epsilon = 1e-30
highest = lax.Precision.HIGHEST


def per_device(activations, out_grads, basis, row_moment, col_moment):
    grads_all = lax.all_gather(out_grads, "row", axis=0, tiled=True)
    gradient = lax.dot_general(
        lax.all_gather(activations, "col", axis=0, tiled=True),
        grads_all,
        (((0,), (0,)), ((), ())),
        preferred_element_type=jnp.float32,
    )
    columns = basis
    projected = lax.psum_scatter(
        lax.dot_general(columns, gradient, (((0,), (0,)), ((), ())), precision=highest),
        "row",
        scatter_dimension=0,
        tiled=True,
    )
    squares = projected * projected + epsilon
    col_total = lax.psum(jnp.sum(squares, axis=0), "row")
    row_total = lax.psum(jnp.sum(squares, axis=1), "col")
    row_next = beta_two * row_moment + (1.0 - beta_two) * (row_total / F)
    col_next = beta_two * col_moment + (1.0 - beta_two) * (col_total / R)
    row_mean = lax.psum(jnp.sum(row_next), "row") / R
    second = row_next[:, None] * col_next[None, :] / row_mean
    normalized = projected / jnp.sqrt(second)
    columns = basis
    summed = jnp.dot(
        columns, lax.all_gather(normalized, "row", axis=0, tiled=True), precision=highest
    )
    weight_update = scale_alpha * summed
    return (weight_update, row_next, col_next)


def solution(mesh):
    in_specs = (P("col", "row"), P("row", "col"), P("row", None), P("row"), P("col"))
    out_specs = (P("row", "col"), P("row"), P("col"))
    return jax.shard_map(
        per_device, mesh=mesh, in_specs=in_specs, out_specs=out_specs, check_vma=False
    )
```

profile of v0, /device:TPU:1, one launch (start us, length us, event | category | flops | bytes accessed | tf_op | source)
XLA Modules:
  0.0 334.7 jit_solution(14622385694253535906)
XLA Ops:
  7.2 0.0 copy-start
  7.2 0.0 all-gather.6.cloned.1.call-start
  7.2 0.7 all-gather.6.cloned.1.call-update
  7.9 0.0 all-gather.4.cloned.1.call-start
  8.0 0.7 all-gather.4.cloned.1.call-update
  8.7 0.0 reduce-scatter.4.cloned.1.call-start
  8.7 46.1 %all-gather.6.cloned.1.call-done = bf16[4096,688]{0,1:T(8,128)(2,1)} async-done(((bf16[512,688]{0,1:T(8,128)(2,1)}), bf16[4096,688]{0,1:T(8,128)(2,1)}) %all-gather.6.cloned.1.call-update) | async-done | bytes 5636112 | tf_op jit(solution)/shard_map/all_gather | solution.py:17
  54.8 100.4 %all-gather.4.cloned.1.call-done = bf16[4096,1024]{1,0:T(8,128)(2,1)} async-done(((bf16[128,1024]{1,0:T(8,128)(2,1)}), bf16[4096,1024]{1,0:T(8,128)(2,1)}) %all-gather.4.cloned.1.call-update) | async-done | bytes 8388624 | tf_op jit(solution)/shard_map/all_gather | solution.py:19
  155.2 10.0 %fusion.3 = f32[1024,688]{0,1:T(8,128)S(1)} fusion(bf16[4096,688]{0,1:T(8,128)(2,1)} %all-gather.6.cloned.1.call-done, bf16[4096,1024]{1,0:T(8,128)(2,1)} %all-gather.4.cloned.1.call-done), kind=kOutput, calls=%fused_computation.9 | convolution fusion | flops 5771362304 | bytes 16842752 | tf_op jit(solution)/shard_map/dot_general | solution.py:18
  165.2 4.6 %convolution_bitcast_fusion = f32[512,688]{0,1:T(8,128)S(1)} fusion(f32[1024,688]{0,1:T(8,128)S(1)} %fusion.3, f32[1024,512]{1,0:T(8,128)S(1)} %copy-done), kind=kOutput, calls=%fused_computation.1 | convolution fusion | flops 4328521728 | bytes 6324224 | tf_op jit(solution)/shard_map/dot_general | solution.py:26
  169.9 0.0 copy-start.2
  169.9 1.6 copy.10
  171.5 0.0 reduce-scatter.4.cloned.1.call-update
  171.5 0.0 all-gather.8.cloned.1.call-start
  171.6 30.3 %reduce-scatter.4.cloned.1.call-done = f32[64,688]{1,0:T(8,128)} async-done(((f32[512,688]{1,0:T(8,128)}), f32[64,688]{1,0:T(8,128)}) %reduce-scatter.4.cloned.1.call-update) | async-done | bytes 176144 | tf_op jit(solution)/shard_map/reduce_scatter | solution.py:25
  201.9 1.1 copy.11
  203.0 0.2 fusion
  203.2 60.8 %psum.21 = f32[64]{0:T(128)S(1)} all-reduce(f32[64]{0:T(128)S(1)} %get-tuple-element.4), channel_id=1, replica_groups=mesh['row'=8,'col'=32] {'col'}, use_global_device_ids=true, to_apply=%region_2.0 | all-reduce | flops 64 | bytes 512 | tf_op jit(solution)/shard_map/psum | solution.py:33
  263.9 0.6 fusion.2
  264.6 30.0 %all-reduce = (f32[]{:T(128)}, f32[688]{0:T(1024)S(1)}) all-reduce(f32[]{:T(128)} %get-tuple-element.7, f32[688]{0:T(1024)S(1)} %get-tuple-element.3), channel_id=1, replica_groups=mesh['row'=8,'col'=32] {'row'}, use_global_device_ids=true, to_apply=%region_6.0 | all-reduce | flops 689 | bytes 5512 | tf_op jit(solution)/shard_map/psum | solution.py:36
  295.2 1.7 rsqrt_multiply_fusion
  296.9 0.0 all-gather.8.cloned.1.call-update
  297.0 18.2 %all-gather.8.cloned.1.call-done = f32[512,688]{1,0:T(8,128)} async-done(((f32[64,688]{1,0:T(8,128)}), f32[512,688]{1,0:T(8,128)}) %all-gather.8.cloned.1.call-update) | async-done | bytes 1409040 | tf_op jit(solution)/shard_map/all_gather | solution.py:41
  315.2 12.9 %multiply_bitcast_fusion = f32[1024,688]{0,1:T(8,128)} fusion(f32[512,688]{1,0:T(8,128)} %all-gather.8.cloned.1.call-done, f32[1024,512]{1,0:T(8,128)S(1)} %copy-done), kind=kOutput, calls=%fused_computation | convolution fusion | flops 4329226240 | bytes 6324224 | tf_op jit(solution)/shard_map/dot_general | solution.py:40
  (9 shorter events, 0.0 us)
Async XLA Ops:
  7.2 158.1 %copy-start = (f32[1024,512]{1,0:T(8,128)S(1)}, f32[1024,512]{1,0:T(8,128)}, u32[]{:S(2)}) copy-start(f32[1024,512]{1,0:T(8,128)} %param.7) | copy-start | bytes 6291460
  7.2 47.6 %all-gather.6.cloned.1.call-start = ((), (), s32[]{:S(2)}) async-start(), calls=%async_computation.2 | async-start | bytes 6340608 | tf_op jit(solution)/shard_map/all_gather | solution.py:17
  7.9 147.3 %all-gather.4.cloned.1.call-start = ((), (), s32[]{:S(2)}) async-start(), calls=%async_computation.1 | async-start | bytes 8650752 | tf_op jit(solution)/shard_map/all_gather | solution.py:19
  8.7 193.2 %reduce-scatter.4.cloned.1.call-start = ((), (), s32[]{:S(2)}) async-start(), calls=%async_computation.4 | async-start | bytes 1769472 | tf_op jit(solution)/shard_map/reduce_scatter | solution.py:25
  169.9 94.1 %copy-start.4 = (f32[64]{0:T(128)S(1)}, f32[64]{0:T(128)}, u32[]{:S(2)}) copy-start(f32[64]{0:T(128)} %param.8) | copy-start | bytes 772
  169.9 125.3 %copy-start.2 = (f32[688]{0:T(1024)S(1)}, f32[688]{0:T(1024)}, u32[]{:S(2)}) copy-start(f32[688]{0:T(1024)} %param.9) | copy-start | bytes 8260
  171.5 143.7 %all-gather.8.cloned.1.call-start = ((), (), s32[]{:S(2)}) async-start(), calls=%async_computation.3 | async-start | bytes 1769472 | tf_op jit(solution)/shard_map/all_gather | solution.py:41
  264.6 63.6 %copy-start.3 = (f32[64]{0:T(128)}, f32[64]{0:T(128)S(1)}, u32[]{:S(2)}) copy-start(f32[64]{0:T(128)S(1)} %get-tuple-element.8) | copy-start | bytes 772
  295.2 32.9 %copy-start.1 = (f32[688]{0:T(1024)}, f32[688]{0:T(1024)S(1)}, u32[]{:S(2)}) copy-start(f32[688]{0:T(1024)S(1)} %multiply_add_fusion.1) | copy-start | bytes 8260
Sparse Core Ops, SparseCore 0:
  9.9 44.8 all-gather.5
  57.4 97.7 all-gather.3
  171.6 30.1 reduce-scatter.3
  297.1 18.0 all-gather.7
where the time goes:
time: 335 us
  waiting for transfers between devices  196 us (59%)
  blocking collectives  90.8 us (27%)
  matrix products  27.6 us (8%)
  between operations  14.5 us (4%)
    all_gather x1, waiting for transfers between devices, per_device(): lax.all_gather(activations, 'col', axis=0, tiled=True)  100 us
    psum x1, blocking collectives, per_device(): row_total = lax.psum(jnp.sum(squares, axis=1), 'col')  60.8 us
    all_gather x1, waiting for transfers between devices, per_device(): grads_all = lax.all_gather(out_grads, 'row', axis=0, tiled=True)  46.1 us
    reduce_scatter x1, waiting for transfers between devices, per_device(): lax.psum_scatter(lax.dot_general(columns, gradient, (((0,), (0,)), ((), (...  30.3 us
    psum x1, blocking collectives, per_device(): row_mean = lax.psum(jnp.sum(row_next), 'row') / R  30 us
    all_gather x1, waiting for transfers between devices, per_device(): lax.all_gather(normalized, 'row', axis=0, tiled=True)  18.2 us
    dot_general x1, matrix products, per_device(): jnp.dot(columns, lax.all_gather(normalized, 'row', axis=0, tiled=True), p...  12.9 us
    dot_general x1, matrix products, per_device(): lax.dot_general(lax.all_gather(activations, 'col', axis=0, tiled=True), g...  10 us
  transfers between devices with their start and end apart: 4, of which 4 were waited for; matrix products, arithmetic and copies ran while one was open for 0% of the time, Pallas kernels for 0%

commit v1 on v0

v1 whole, which is shorter than its diff:
```python
import jax
import jax.numpy as jnp
from jax import lax
from jax.experimental import pallas as pl
from jax.experimental.pallas import tpu as pltpu
from jax.sharding import PartitionSpec as P

F = 22016
R = 512
MESH = pl.DeviceIdType.MESH
f32 = jnp.float32
bf16 = jnp.bfloat16

beta_two = 0.8
scale_alpha = 0.25
epsilon = 1e-30

NX, NY, NZ = 4, 4, 8
ROWS = 2 * NX
COLS = NY * NZ
RB = R // ROWS
TB = 128
TG = 512
FB = F // COLS
LIFT = 2.0 ** 7.875


def split(v):
    high = v.astype(bf16)
    return high, (v - high.astype(f32)).astype(bf16)


def encode(u):
    top = jnp.maximum(jnp.max(jnp.abs(u), axis=0, keepdims=True), 1e-30)
    w = u * (LIFT / top)
    w = w * w
    w = w * w
    w = w * w
    w = w * w
    return jnp.where(u < 0, -w, w).astype(bf16), top * (1.0 / LIFT)


def decode(code, unit):
    t = code.astype(f32)
    m = jnp.exp2(jnp.log2(jnp.abs(t)) * 0.0625)
    m = jnp.where(t == 0, 0.0, m)
    return jnp.where(t < 0, -m, m) * unit


def kernel(act, grads, basis, rm, cm, w_out, rn_out, cn_out,
           a_v, b_v, g_v, sp, srecv, senc, sunit, sall, uall, shl, acc,
           penc, punit, rst, rsall, rnown, rnall, p_h, p_l, w_v,
           ld, s1s, s1r, bds, bdr, bus, bur, gs, gfs, gpr, gmr, g2r, gss, gsr,
           pds, pdr, pus, pur, sps, spr, sus, sur, rss, rsr, rns, rnr, wsem, ysem):
    row, col = lax.axis_index("row"), lax.axis_index("col")
    x, k = row // 2, row % 2
    y, z = col // NZ, col % NZ

    def at_x(o):
        return (lax.rem(x + o + NX, NX) * 2 + k, col)

    sibling = (x * 2 + 1 - k, col)

    def send(src, dst, ssem, rsem, dev):
        pltpu.make_async_remote_copy(src_ref=src, dst_ref=dst, send_sem=ssem, recv_sem=rsem,
                                     device_id=dev, device_id_type=MESH).start()

    def arrived(ref, sem):
        pltpu.make_async_copy(ref, ref, sem).wait()

    load_b = pltpu.make_async_copy(basis, b_v, ld.at[0])
    load_a = pltpu.make_async_copy(act, a_v, ld.at[1])
    load_g = pltpu.make_async_copy(grads, g_v.at[row], ld.at[2])
    load_b.start()
    load_a.start()
    load_g.start()

    barrier = pltpu.get_barrier_semaphore()
    for i in range(1, ROWS):
        pl.semaphore_signal(barrier, inc=1, device_id=(lax.rem(row + i, ROWS), col), device_id_type=MESH)
    for i in range(1, NZ):
        pl.semaphore_signal(barrier, inc=1, device_id=(row, y * NZ + lax.rem(z + i, NZ)), device_id_type=MESH)
    for i in range(1, NY):
        pl.semaphore_signal(barrier, inc=1, device_id=(row, lax.rem(y + i, NY) * NZ + z), device_id_type=MESH)

    load_b.wait()
    load_a.wait()
    b_h, b_l = split(b_v[...])
    a = a_v[...]
    part = jnp.dot(a, b_h, preferred_element_type=f32) + jnp.dot(a, b_l, preferred_element_type=f32)
    sp[...] = part.T.reshape(ROWS, RB, TB)
    load_g.wait()
    pl.semaphore_wait(barrier, ROWS + NZ + NY - 3)

    for i in range(1, ROWS):
        peer = lax.rem(row + i, ROWS)
        send(sp.at[peer], srecv.at[i], s1s.at[i], s1r.at[i], (peer, col))
    for i in range(1, NY):
        pl.semaphore_signal(ysem, inc=1, device_id=(row, lax.rem(y + i, NY) * NZ + z), device_id_type=MESH)

    H = TG // 2
    for h in range(2):
        lo, hi = pl.ds(h * H, H), pl.ds((1 - h) * H, H)
        send(g_v.at[row, lo], g_v.at[row, lo], gs.at[h], gpr.at[h], at_x(1))
        send(g_v.at[row, hi], g_v.at[row, hi], gs.at[2 + h], gmr.at[1 - h], at_x(-1))
    send(g_v.at[row], g_v.at[row], gss.at[0], gsr.at[0], sibling)

    total = sp[row]
    for i in range(1, ROWS):
        arrived(srecv.at[i], s1r.at[i])
        total = total + srecv[i]
    code, unit = encode(total)
    senc[...] = code
    sunit[...] = unit
    sall[col] = code
    uall[col] = unit
    pl.semaphore_wait(ysem, NY - 1)

    @pl.loop(1, COLS)
    def _(i):
        peer = lax.rem(col + i, COLS)
        send(senc, sall.at[col], bds.at[i], bdr.at[i], (row, peer))
        send(sunit, uall.at[col], bus.at[i], bur.at[i], (row, peer))

    before = lax.rem(x + NX - 1, NX) * 2 + k
    after = lax.rem(x + 1, NX) * 2 + k
    across = lax.rem(x + 2, NX) * 2 + k
    h0, h1 = pl.ds(0, H), pl.ds(H, H)
    arrived(g_v.at[before, h0], gpr.at[0])
    send(g_v.at[before, h0], g_v.at[before, h0], gfs.at[0], g2r.at[0], at_x(1))
    arrived(g_v.at[after, h1], gmr.at[1])
    send(g_v.at[after, h1], g_v.at[after, h1], gfs.at[1], g2r.at[1], at_x(-1))
    send(g_v.at[before, h0], g_v.at[before, h0], gss.at[1], gsr.at[1], sibling)
    send(g_v.at[after, h1], g_v.at[after, h1], gss.at[2], gsr.at[2], sibling)
    arrived(g_v.at[before, h1], gpr.at[1])
    send(g_v.at[before, h1], g_v.at[before, h1], gss.at[3], gsr.at[3], sibling)
    arrived(g_v.at[after, h0], gmr.at[0])
    send(g_v.at[after, h0], g_v.at[after, h0], gss.at[4], gsr.at[4], sibling)

    @pl.loop(1, COLS)
    def _(i):
        arrived(senc, bdr.at[i])
        arrived(sunit, bur.at[i])

    @pl.loop(0, ROWS)
    def _(r):
        for j in range(TG // TB):
            high, low = split(decode(sall[r * (TG // TB) + j], uall[r * (TG // TB) + j]))
            shl[r, 0:RB, j * TB:(j + 1) * TB] = high
            shl[r, RB:2 * RB, j * TB:(j + 1) * TB] = low

    def project(r):
        return jnp.dot(shl[r], g_v[r], preferred_element_type=f32)

    acc[...] = project(row)
    acc[...] += project(before)
    acc[...] += project(after)
    arrived(g_v.at[row], gsr.at[0])
    other = 1 - 2 * k
    acc[...] += project(row + other)
    arrived(g_v.at[before, h0], gsr.at[1])
    arrived(g_v.at[before, h0], gsr.at[3])
    acc[...] += project(before + other)
    arrived(g_v.at[before, h0], gsr.at[2])
    arrived(g_v.at[before, h0], gsr.at[4])
    acc[...] += project(after + other)
    arrived(g_v.at[across, h0], g2r.at[0])
    send(g_v.at[across, h0], g_v.at[across, h0], gss.at[5], gsr.at[5], sibling)
    arrived(g_v.at[across, h1], g2r.at[1])
    send(g_v.at[across, h1], g_v.at[across, h1], gss.at[6], gsr.at[6], sibling)
    acc[...] += project(across)
    arrived(g_v.at[across, h0], gsr.at[5])
    arrived(g_v.at[across, h1], gsr.at[6])
    acc[...] += project(across + other)

    mine = acc[0:RB] + acc[RB:2 * RB]
    code, unit = encode(mine)
    penc[row] = code
    punit[row] = unit
    for i in range(1, NX):
        send(penc.at[row], penc.at[row], pds.at[i], pdr.at[i], at_x(i))
        send(punit.at[row], punit.at[row], pus.at[i], pur.at[i], at_x(i))
    send(penc.at[row], penc.at[row], sps.at[0], spr.at[0], sibling)
    send(punit.at[row], punit.at[row], sus.at[0], sur.at[0], sibling)

    squares = mine * mine + epsilon
    none = jnp.zeros_like(squares)
    wide = jnp.where(k == 0, jnp.concatenate([squares, none], axis=0), jnp.concatenate([none, squares], axis=0))
    sums = lax.dot_general(jnp.ones((8, FB), f32), wide, (((1,), (1,)), ((), ())),
                           precision=lax.Precision.HIGHEST, preferred_element_type=f32)
    rst[...] = sums[0:1]
    rsall[col] = sums[0:1]

    @pl.loop(1, COLS)
    def _(i):
        send(rst, rsall.at[col], rss.at[i], rsr.at[i], (row, lax.rem(col + i, COLS)))

    @pl.loop(1, COLS)
    def _(i):
        arrived(rst, rsr.at[i])

    lane = lax.broadcasted_iota(jnp.int32, (1, 2 * RB), 1)
    old = jnp.concatenate([rm[...], rm[...]], axis=1)
    row_next = beta_two * old + (1.0 - beta_two) * (jnp.sum(rsall[...], axis=0) / F)
    rn_out[...] = jnp.where(k == 0, row_next[:, 0:RB], row_next[:, RB:2 * RB])
    row_next = jnp.where(lane // RB == k, row_next, 0.0)
    rnown[...] = row_next
    rnall[row] = row_next
    for i in range(1, ROWS):
        send(rnown, rnall.at[row], rns.at[i], rnr.at[i], (lax.rem(row + i, ROWS), col))

    for i in (1, 3, 2):
        piece = lax.rem(x + NX - i, NX) * 2 + k
        arrived(penc.at[piece], pdr.at[i])
        send(penc.at[piece], penc.at[piece], sps.at[i], spr.at[i], sibling)
        arrived(punit.at[piece], pur.at[i])
        send(punit.at[piece], punit.at[piece], sus.at[i], sur.at[i], sibling)
    for i in range(NX):
        arrived(penc.at[row], spr.at[i])
        arrived(punit.at[row], sur.at[i])

    col_sum = jnp.zeros((1, FB), f32)
    for r in range(ROWS):
        u = decode(penc[r], punit[r])
        col_sum = col_sum + jnp.sum(u * u + epsilon, axis=0, keepdims=True)
        high, low = split(u)
        p_h[r * RB:(r + 1) * RB, :] = high
        p_l[r * RB:(r + 1) * RB, :] = low
    col_next = beta_two * cm[...] + (1.0 - beta_two) * (col_sum / R)
    cn_out[...] = col_next

    for i in range(1, ROWS):
        arrived(rnown, rnr.at[i])
    rows = jnp.concatenate([rnall[2 * i] + rnall[2 * i + 1] for i in range(NX)], axis=1)
    by_row = 1.0 / jnp.sqrt(rows)
    row_mean = jnp.sum(rows, axis=1, keepdims=True) / R
    by_col = scale_alpha * jnp.sqrt(row_mean) / jnp.sqrt(col_next)
    M = 256
    for m in range(4):
        high, low = split(b_v[m * M:(m + 1) * M, :] * by_row)
        w = jnp.dot(high, p_h[...], preferred_element_type=f32)
        w += jnp.dot(high, p_l[...], preferred_element_type=f32)
        w += jnp.dot(low, p_h[...], preferred_element_type=f32)
        w_v[m * M:(m + 1) * M, :] = w * by_col
        pltpu.make_async_copy(w_v.at[pl.ds(m * M, M)], w_out.at[pl.ds(m * M, M)], wsem.at[m]).start()

    for i in range(1, ROWS):
        arrived(srecv.at[i], s1s.at[i])
        arrived(rnown, rns.at[i])

    @pl.loop(1, COLS)
    def _(i):
        arrived(senc, bds.at[i])
        arrived(sunit, bus.at[i])
        arrived(rst, rss.at[i])
    for i in range(4):
        arrived(g_v.at[row, h0], gs.at[i])
    for i in range(2):
        arrived(g_v.at[row, h0], gfs.at[i])
    arrived(g_v.at[row], gss.at[0])
    for i in range(1, 7):
        arrived(g_v.at[row, h0], gss.at[i])
    for i in range(NX):
        arrived(penc.at[row], sps.at[i])
        arrived(punit.at[row], sus.at[i])
    for i in range(1, NX):
        arrived(penc.at[row], pds.at[i])
        arrived(punit.at[row], pus.at[i])
    for m in range(4):
        pltpu.make_async_copy(w_v.at[pl.ds(m * M, M)], w_out.at[pl.ds(m * M, M)], wsem.at[m]).wait()


def per_device(activations, out_grads, basis, row_moment, col_moment):
    any_spec = pl.BlockSpec(memory_space=pl.ANY)
    vmem = pl.BlockSpec(memory_space=pltpu.VMEM)
    dma = pltpu.SemaphoreType.DMA
    w, rn, cn = pl.pallas_call(
        kernel,
        out_shape=(
            jax.ShapeDtypeStruct((1024, FB), f32),
            jax.ShapeDtypeStruct((1, RB), f32),
            jax.ShapeDtypeStruct((1, FB), f32),
        ),
        in_specs=[any_spec, any_spec, any_spec, vmem, vmem],
        out_specs=(any_spec, vmem, vmem),
        scratch_shapes=[
            pltpu.VMEM((TB, 1024), bf16),
            pltpu.VMEM((1024, R), f32),
            pltpu.VMEM((ROWS, TG, FB), bf16),
            pltpu.VMEM((ROWS, RB, TB), f32),
            pltpu.VMEM((ROWS, RB, TB), f32),
            pltpu.VMEM((RB, TB), bf16),
            pltpu.VMEM((1, TB), f32),
            pltpu.VMEM((COLS, RB, TB), bf16),
            pltpu.VMEM((COLS, 1, TB), f32),
            pltpu.VMEM((ROWS, 2 * RB, TG), bf16),
            pltpu.VMEM((2 * RB, FB), f32),
            pltpu.VMEM((ROWS, RB, FB), bf16),
            pltpu.VMEM((ROWS, 1, FB), f32),
            pltpu.VMEM((1, 2 * RB), f32),
            pltpu.VMEM((COLS, 1, 2 * RB), f32),
            pltpu.VMEM((1, 2 * RB), f32),
            pltpu.VMEM((ROWS, 1, 2 * RB), f32),
            pltpu.VMEM((R, FB), bf16),
            pltpu.VMEM((R, FB), bf16),
            pltpu.VMEM((1024, FB), f32),
            dma((3,)),
            dma((ROWS,)), dma((ROWS,)),
            dma((COLS,)), dma((COLS,)), dma((COLS,)), dma((COLS,)),
            dma((4,)), dma((2,)), dma((2,)), dma((2,)), dma((2,)), dma((7,)), dma((7,)),
            dma((NX,)), dma((NX,)), dma((NX,)), dma((NX,)),
            dma((NX,)), dma((NX,)), dma((NX,)), dma((NX,)),
            dma((COLS,)), dma((COLS,)),
            dma((ROWS,)), dma((ROWS,)),
            dma((4,)),
            pltpu.SemaphoreType.REGULAR,
        ],
        compiler_params=pltpu.CompilerParams(
            collective_id=0, has_side_effects=True, vmem_limit_bytes=48 * 2**20
        ),
    )(activations, out_grads, basis, row_moment.reshape(1, RB), col_moment.reshape(1, FB))
    return w, rn.reshape(RB), cn.reshape(FB)


def solution(mesh):
    in_specs = (P("col", "row"), P("row", "col"), P("row", None), P("row"), P("col"))
    out_specs = (P("row", "col"), P("row"), P("col"))
    return jax.shard_map(
        per_device, mesh=mesh, in_specs=in_specs, out_specs=out_specs, check_vma=False
    )
```

time: 335 us -> 69.1 us (0.21)
  waiting for transfers between devices: 196 us -> 0 us
  blocking collectives: 90.8 us -> 0 us
  Pallas kernels: 0 us -> 58.4 us
  matrix products: 27.6 us -> 0 us
  between operations: 14.5 us -> 0.66 us
  local copies, waits for them, and re-layouts: 2.74 us -> 9.2 us
    all_gather x3 -> x0, waiting for transfers between devices: 165 us -> none  [the longest x1 100 us: per_device(): lax.all_gather(activations, 'col', axis=0, tiled=True)]
    psum x2 -> x0, blocking collectives: 90.8 us -> none  [the longest x1 60.8 us: per_device(): row_total = lax.psum(jnp.sum(squares, axis=1), 'col')]
    pallas_call x0 -> x1, Pallas kernels: none -> 58.4 us  [per_device(): pl.pallas_call(kernel, out_shape=(jax.ShapeDtypeStruct((1024, FB), f32),...]
    reduce_scatter x1 -> x0, waiting for transfers between devices: 30.3 us -> none  [per_device(): lax.psum_scatter(lax.dot_general(columns, gradient, (((0,), (0,)), ((), (...]
    dot_general x3 -> x0, matrix products: 27.6 us -> none  [the longest x1 12.9 us: per_device(): jnp.dot(columns, lax.all_gather(normalized, 'row', axis=0, tiled=True), p...]
    unnamed x12 -> x9, local copies, waits for them, and re-layouts: 2.74 us -> 8.51 us
  transfers between devices with their start and end apart: 4 -> 0, of which waited for: 4 -> 0; matrix products, arithmetic and copies ran while one was open for 0% -> 0% of each run, Pallas kernels for 0% -> 0%
where the time goes in v1:
time: 69.1 us; the launch traced here: 68.9 us
  Pallas kernels  58.4 us (85%)
  local copies, waits for them, and re-layouts  9.2 us (13%)
    pallas_call x1, Pallas kernels, per_device(): pl.pallas_call(kernel, out_shape=(jax.ShapeDtypeStruct((1024, FB), f32),...  58.4 us
    unnamed x9, local copies, waits for them, and re-layouts  8.51 us

profile of v1, /device:TPU:1, one launch (start us, length us, event | category | flops | bytes accessed | tf_op | source)
XLA Modules:
  0.0 68.9 jit_solution(3918543296137151831)
XLA Ops:
  0.6 0.7 %reshape.19.cm = f32[1,688]{1,0:T(1,128)S(1)} reshape(f32[688]{0:T(1024)} %param.9) | data formatting | bytes 5504 | tf_op jit(solution)/shard_map/reshape | solution.py:321
  1.3 1.4 %copy.8.grads = bf16[512,688]{1,0:T(8,128)(2,1)S(1)} copy(bf16[512,688]{0,1:T(8,128)(2,1)} %param.6) | data formatting | bytes 1409024 | tf_op args[1]
  2.7 0.0 copy-start
  2.7 1.6 %copy-done = f32[1024,512]{1,0:T(8,128)S(1)} copy-done((f32[1024,512]{1,0:T(8,128)S(1)}, f32[1024,512]{1,0:T(8,128)}, u32[]{:S(2)}) %copy-start) | copy-done | bytes 2097176
  4.3 0.0 copy-start.1
  4.3 0.9 %copy-done.1 = bf16[128,1024]{1,0:T(8,128)(2,1)S(1)} copy-done((bf16[128,1024]{1,0:T(8,128)(2,1)S(1)}, bf16[128,1024]{1,0:T(8,128)(2,1)}, u32[]{:S(2)}) %copy-start.1) | copy-done | bytes 262168
  5.2 0.0 copy-start.2
  5.2 0.7 copy-done.2
  5.9 58.4 %shard_map.76 = (f32[1024,688]{1,0:T(8,128)}, f32[1,64]{1,0:T(1,128)S(1)}, f32[1,688]{1,0:T(1,128)S(1)}) custom-call(bf16[128,1024]{1,0:T(8,128)(2,1)S(1)} %copy-done.1, bf16[512,688]{1,0:T(8,128)(2,1)S(1)} %copy.8.grads, f32[1024,512]{1,0:T(8,128)S(1)} %copy-done, f32[1,64]{1,0:T(1,128)S(1)} %bitcast.2, f32[1,688]{1,0:T(1,128)S(1)} %reshape.19.cm), custom_call_target="tpu_custom_call" | custom-call | tf_op jit(solution)/shard_map/pallas_call | solution.py:277
  64.3 3.4 %copy.9 = f32[1024,688]{0,1:T(8,128)} copy(f32[1024,688]{1,0:T(8,128)} %get-tuple-element.9) | data formatting | bytes 5636096
  67.8 0.6 reduce
  68.4 0.5 copy.11
Async XLA Ops:
  2.7 1.6 %copy-start = (f32[1024,512]{1,0:T(8,128)S(1)}, f32[1024,512]{1,0:T(8,128)}, u32[]{:S(2)}) copy-start(f32[1024,512]{1,0:T(8,128)} %basis.1) | copy-start | bytes 6291460
  4.3 0.9 %copy-start.1 = (bf16[128,1024]{1,0:T(8,128)(2,1)S(1)}, bf16[128,1024]{1,0:T(8,128)(2,1)}, u32[]{:S(2)}) copy-start(bf16[128,1024]{1,0:T(8,128)(2,1)} %act.1) | copy-start | bytes 786436
  5.2 0.7 copy-start.2

commit v2 on v1

v2 whole, which is shorter than its diff:
```python
import jax
import jax.numpy as jnp
from jax import lax
from jax.experimental import pallas as pl
from jax.experimental.pallas import tpu as pltpu
from jax.sharding import PartitionSpec as P

F = 22016
R = 512
MESH = pl.DeviceIdType.MESH
f32 = jnp.float32
bf16 = jnp.bfloat16

beta_two = 0.8
scale_alpha = 0.25
epsilon = 1e-30

NX, NY, NZ = 4, 4, 8
ROWS = 2 * NX
COLS = NY * NZ
RB = R // ROWS
RC = 2 * RB
TB = 128
TG = 512
DB = 1024
FB = F // COLS
FH = 352
LIFT = 2.0 ** 7.875


def split(v):
    high = v.astype(bf16)
    return high, (v - high.astype(f32)).astype(bf16)


def encode(u):
    top = jnp.maximum(jnp.max(jnp.abs(u), axis=0, keepdims=True), 1e-30)
    w = u * (LIFT / top)
    w = w * w
    w = w * w
    w = w * w
    w = w * w
    return jnp.where(u < 0, -w, w).astype(bf16), top * (1.0 / LIFT)


def decode(code, unit):
    t = code.astype(f32)
    m = jnp.exp2(jnp.log2(jnp.abs(t)) * 0.0625)
    m = jnp.where(t == 0, 0.0, m)
    return jnp.where(t < 0, -m, m) * unit


def exchange(act, grads, basis, rm, u_out, rows_out, rn_out, bh_out, bl_out,
             a_v, b_v, rm_v, g_own, g_v, sp, srecv, senc, sunit, sall, uall, shl, acc,
             penc, punit, rst, rsall, rnown, rnall,
             ld, s1s, s1r, bds, bdr, bus, bur, gps, gms, gfs, gpr, gmr, g2r, gss, gsr, sss, ssr,
             pds, pdr, pus, pur, sps, spr, sus, sur, rss, rsr, rns, rnr, ysem):
    row, col = lax.axis_index("row"), lax.axis_index("col")
    x, k = row // 2, row % 2
    y, z = col // NZ, col % NZ

    def at_x(o, core):
        return (lax.rem(x + o + NX, NX) * 2 + core, col)

    sibling = (x * 2 + 1 - k, col)

    def send(src, dst, ssem, rsem, dev):
        pltpu.make_async_remote_copy(src_ref=src, dst_ref=dst, send_sem=ssem, recv_sem=rsem,
                                     device_id=dev, device_id_type=MESH).start()

    def arrived(ref, sem):
        pltpu.make_async_copy(ref, ref, sem).wait()

    loads = [
        pltpu.make_async_copy(basis, b_v, ld.at[0]),
        pltpu.make_async_copy(act, a_v, ld.at[1]),
        pltpu.make_async_copy(grads.at[pl.ds(0, FH)], g_own.at[0], ld.at[2]),
        pltpu.make_async_copy(grads.at[pl.ds(FH, FB - FH)], g_own.at[1, pl.ds(0, FB - FH)], ld.at[3]),
        pltpu.make_async_copy(rm, rm_v, ld.at[4]),
    ]
    for load in loads:
        load.start()

    barrier = pltpu.get_barrier_semaphore()
    for i in range(1, ROWS):
        pl.semaphore_signal(barrier, inc=1, device_id=(lax.rem(row + i, ROWS), col), device_id_type=MESH)
    for i in range(1, NZ):
        pl.semaphore_signal(barrier, inc=1, device_id=(row, y * NZ + lax.rem(z + i, NZ)), device_id_type=MESH)
    for i in range(1, NY):
        pl.semaphore_signal(barrier, inc=1, device_id=(row, lax.rem(y + i, NY) * NZ + z), device_id_type=MESH)
    g_own[1, FB - FH:FH, :] = jnp.zeros((2 * FH - FB, TG), bf16)

    loads[0].wait()
    loads[1].wait()
    b_h, b_l = split(b_v[...])
    a = a_v[...]
    part = jnp.dot(a, b_h, preferred_element_type=f32) + jnp.dot(a, b_l, preferred_element_type=f32)
    sp[...] = part.T.reshape(ROWS, RB, TB)
    for load in loads[2:]:
        load.wait()
    pl.semaphore_wait(barrier, ROWS + NZ + NY - 3)

    for i in range(1, ROWS):
        peer = lax.rem(row + i, ROWS)
        send(sp.at[peer], srecv.at[i], s1s.at[i], s1r.at[i], (peer, col))
    for i in range(1, NY):
        pl.semaphore_signal(ysem, inc=1, device_id=(row, lax.rem(y + i, NY) * NZ + z), device_id_type=MESH)

    def send_up():
        for core in range(2):
            send(g_own.at[core], g_v.at[row], gps.at[core], gpr.at[k], at_x(1, core))

    def send_down():
        for core in range(2):
            send(g_own.at[core], g_v.at[row], gms.at[core], gmr.at[k], at_x(-1, core))

    send_up()
    send_down()
    send(g_own.at[1 - k], g_v.at[row], gss, gsr, sibling)

    total = sp[row]
    for i in range(1, ROWS):
        arrived(srecv.at[i], s1r.at[i])
        total = total + srecv[i]
    code, unit = encode(total)
    senc[...] = code
    sunit[...] = unit
    sall[k, col] = code
    uall[k, col] = unit
    pl.semaphore_wait(ysem, NY - 1)

    @pl.loop(1, COLS)
    def _(i):
        peer = lax.rem(col + i, COLS)
        send(senc, sall.at[k, col], bds.at[i], bdr.at[i], (row, peer))
        send(sunit, uall.at[k, col], bus.at[i], bur.at[i], (row, peer))

    before = lax.rem(x + NX - 1, NX) * 2
    after = lax.rem(x + 1, NX) * 2
    across = lax.rem(x + 2, NX) * 2
    arrived(g_v.at[before], gpr.at[0])
    send(g_v.at[before], g_v.at[before], gfs.at[0], g2r.at[0], at_x(1, k))
    arrived(g_v.at[after + 1], gmr.at[1])
    send(g_v.at[after + 1], g_v.at[after + 1], gfs.at[1], g2r.at[1], at_x(-1, k))

    turned_h, turned_l = split(b_v[...].T)
    bh_out[...] = turned_h
    bl_out[...] = turned_l

    @pl.loop(1, COLS)
    def _(i):
        arrived(senc, bdr.at[i])
        arrived(sunit, bur.at[i])
    send(sall.at[k], sall.at[k], sss.at[0], ssr.at[0], sibling)
    send(uall.at[k], uall.at[k], sss.at[1], ssr.at[1], sibling)
    arrived(sall.at[k], ssr.at[0])
    arrived(uall.at[k], ssr.at[1])

    @pl.loop(0, ROWS)
    def _(r):
        for j in range(TG // TB):
            b = r * (TG // TB) + j
            for core in range(2):
                high, low = split(decode(sall[core, b], uall[core, b]))
                shl[r, core * RB:(core + 1) * RB, j * TB:(j + 1) * TB] = high
                shl[r, RC + core * RB:RC + (core + 1) * RB, j * TB:(j + 1) * TB] = low

    def project(g, r):
        return lax.dot_general(g, shl[r], (((1,), (1,)), ((), ())), preferred_element_type=f32)

    acc[...] = project(g_own[k], row)
    arrived(g_v.at[row], gsr)
    acc[...] += project(g_v[x * 2 + 1 - k], x * 2 + 1 - k)
    acc[...] += project(g_v[before], before)
    arrived(g_v.at[before], gpr.at[1])
    acc[...] += project(g_v[before + 1], before + 1)
    acc[...] += project(g_v[after + 1], after + 1)
    arrived(g_v.at[after], gmr.at[0])
    acc[...] += project(g_v[after], after)
    arrived(g_v.at[across], g2r.at[0])
    acc[...] += project(g_v[across], across)
    arrived(g_v.at[across], g2r.at[1])
    acc[...] += project(g_v[across + 1], across + 1)

    mine = acc[:, 0:RC] + acc[:, RC:2 * RC]
    code, unit = encode(mine)
    penc[row] = code
    punit[row] = unit
    for i in range(1, NX):
        send(penc.at[row], penc.at[row], pds.at[i], pdr.at[i], at_x(i, k))
        send(punit.at[row], punit.at[row], pus.at[i], pur.at[i], at_x(i, k))
    send(penc.at[row], penc.at[row], sps.at[0], spr.at[0], sibling)
    send(punit.at[row], punit.at[row], sus.at[0], sur.at[0], sibling)

    count = jnp.where(k == 0, float(FH), float(FB - FH))
    sums = jnp.sum(mine * mine, axis=0, keepdims=True) + count * epsilon
    rst[...] = sums
    rsall[col] = sums

    @pl.loop(1, COLS)
    def _(i):
        send(rst, rsall.at[col], rss.at[i], rsr.at[i], (row, lax.rem(col + i, COLS)))

    @pl.loop(1, COLS)
    def _(i):
        arrived(rst, rsr.at[i])

    total = jnp.sum(rsall[...], axis=0)
    old = rm_v[...].reshape(1, RB)
    old = jnp.concatenate([old, old], axis=1)
    lane = lax.broadcasted_iota(jnp.int32, (1, RC), 1)
    mixed = (1.0 - beta_two) * (total / F) + jnp.where(lane // RB == k, beta_two * old, 0.0)
    rnown[...] = mixed
    rnall[row] = mixed
    for i in range(1, ROWS):
        send(rnown, rnall.at[row], rns.at[i], rnr.at[i], (lax.rem(row + i, ROWS), col))

    for i in (1, 3, 2):
        piece = lax.rem(x + NX - i, NX) * 2 + k
        arrived(penc.at[piece], pdr.at[i])
        send(penc.at[piece], penc.at[piece], sps.at[i], spr.at[i], sibling)
        arrived(punit.at[piece], pur.at[i])
        send(punit.at[piece], punit.at[piece], sus.at[i], sur.at[i], sibling)
    for i in range(NX):
        arrived(penc.at[row], spr.at[i])
        arrived(punit.at[row], sur.at[i])
    for r in range(ROWS):
        u_out[(r % 2) * FH:(r % 2 + 1) * FH, (r // 2) * RC:(r // 2 + 1) * RC] = decode(penc[r], punit[r])

    for i in range(1, ROWS):
        arrived(rnown, rnr.at[i])
    for i in range(NX):
        rows_out[:, i * RC:(i + 1) * RC] = rnall[2 * i] + rnall[2 * i + 1]
    chip = rnall[x * 2] + rnall[x * 2 + 1]
    rn_out[...] = jnp.where(k == 0, chip[:, 0:RB], chip[:, RB:RC])

    for i in range(1, ROWS):
        arrived(srecv.at[i], s1s.at[i])
        arrived(rnown, rns.at[i])

    @pl.loop(1, COLS)
    def _(i):
        arrived(senc, bds.at[i])
        arrived(sunit, bus.at[i])
        arrived(rst, rss.at[i])
    for i in range(2):
        arrived(g_v.at[row], gps.at[i])
        arrived(g_v.at[row], gms.at[i])
        arrived(g_v.at[row], gfs.at[i])
    arrived(g_v.at[row], gss)
    arrived(sall.at[k], sss.at[0])
    arrived(uall.at[k], sss.at[1])
    for i in range(NX):
        arrived(penc.at[row], sps.at[i])
        arrived(punit.at[row], sus.at[i])
    for i in range(1, NX):
        arrived(penc.at[row], pds.at[i])
        arrived(punit.at[row], pus.at[i])


MT = 344


def finish(u, rows, rn, bh, bl, cm, w_out, rn_out, cn_out, w_v, cm_v, cn_v, rn_v, sem):
    load = pltpu.make_async_copy(cm, cm_v, sem.at[2])
    load.start()
    rn_v[...] = rn[...].reshape(RB)
    put_rn = pltpu.make_async_copy(rn_v, rn_out, sem.at[3])
    put_rn.start()
    by_row = 1.0 / jnp.sqrt(rows[...])
    row_mean = jnp.sum(rows[...], axis=1, keepdims=True) / R
    top = scale_alpha * jnp.sqrt(row_mean)
    load.wait()
    old = jnp.broadcast_to(cm_v[...].reshape(1, FB), (128, FB)).T
    news = []
    puts = []
    for m in range(2):
        v = u[m * MT:(m + 1) * MT, :]
        col_sum = jnp.sum(v * v + epsilon, axis=1, keepdims=True)
        col_next = beta_two * old[m * MT:(m + 1) * MT] + (1.0 - beta_two) * (col_sum / R)
        news.append(col_next)
        by_col = top / jnp.sqrt(col_next[:, 0:1])
        high, low = split(v * by_row)
        w = jnp.dot(high, bh[...], preferred_element_type=f32)
        w += jnp.dot(low, bh[...], preferred_element_type=f32)
        w += jnp.dot(high, bl[...], preferred_element_type=f32)
        w_v[m * MT:(m + 1) * MT, :] = w * by_col
        put = pltpu.make_async_copy(w_v.at[pl.ds(m * MT, MT)], w_out.at[pl.ds(m * MT, MT)], sem.at[m])
        put.start()
        puts.append(put)
    cn_v[...] = jnp.concatenate(news, axis=0).T[0]
    put_cn = pltpu.make_async_copy(cn_v, cn_out, sem.at[4])
    put_cn.start()
    for put in puts + [put_rn, put_cn]:
        put.wait()


def per_device(activations, out_grads, basis, row_moment, col_moment):
    hbm = pl.BlockSpec(memory_space=pltpu.HBM)
    vmem = pl.BlockSpec(memory_space=pltpu.VMEM)
    dma = pltpu.SemaphoreType.DMA
    u, rows, rn, bh, bl = pl.pallas_call(
        exchange,
        out_shape=(
            jax.ShapeDtypeStruct((2 * FH, R), f32),
            jax.ShapeDtypeStruct((1, R), f32),
            jax.ShapeDtypeStruct((1, RB), f32),
            jax.ShapeDtypeStruct((R, DB), bf16),
            jax.ShapeDtypeStruct((R, DB), bf16),
        ),
        in_specs=[hbm] * 4,
        out_specs=(vmem,) * 5,
        scratch_shapes=[
            pltpu.VMEM((TB, DB), bf16),
            pltpu.VMEM((DB, R), f32),
            pltpu.VMEM((RB,), f32),
            pltpu.VMEM((2, FH, TG), bf16),
            pltpu.VMEM((ROWS, FH, TG), bf16),
            pltpu.VMEM((ROWS, RB, TB), f32),
            pltpu.VMEM((ROWS, RB, TB), f32),
            pltpu.VMEM((RB, TB), bf16),
            pltpu.VMEM((1, TB), f32),
            pltpu.VMEM((2, COLS, RB, TB), bf16),
            pltpu.VMEM((2, COLS, 1, TB), f32),
            pltpu.VMEM((ROWS, 2 * RC, TG), bf16),
            pltpu.VMEM((FH, 2 * RC), f32),
            pltpu.VMEM((ROWS, FH, RC), bf16),
            pltpu.VMEM((ROWS, 1, RC), f32),
            pltpu.VMEM((1, RC), f32),
            pltpu.VMEM((COLS, 1, RC), f32),
            pltpu.VMEM((1, RC), f32),
            pltpu.VMEM((ROWS, 1, RC), f32),
            dma((5,)),
            dma((ROWS,)), dma((ROWS,)),
            dma((COLS,)), dma((COLS,)), dma((COLS,)), dma((COLS,)),
            dma((2,)), dma((2,)), dma((2,)), dma((2,)), dma((2,)), dma((2,)), dma, dma, dma((2,)), dma((2,)),
            dma((NX,)), dma((NX,)), dma((NX,)), dma((NX,)),
            dma((NX,)), dma((NX,)), dma((NX,)), dma((NX,)),
            dma((COLS,)), dma((COLS,)),
            dma((ROWS,)), dma((ROWS,)),
            pltpu.SemaphoreType.REGULAR,
        ],
        compiler_params=pltpu.CompilerParams(
            collective_id=0, has_side_effects=True, vmem_limit_bytes=30 * 2**20
        ),
    )(*[pltpu.with_memory_space_constraint(v, pltpu.HBM) for v in (activations, out_grads.T, basis, row_moment)])
    w, rn, cn = pl.pallas_call(
        finish,
        out_shape=(
            jax.ShapeDtypeStruct((FB, DB), f32),
            jax.ShapeDtypeStruct((RB,), f32),
            jax.ShapeDtypeStruct((FB,), f32),
        ),
        in_specs=[vmem] * 5 + [hbm],
        out_specs=(hbm,) * 3,
        scratch_shapes=[
            pltpu.VMEM((FB, DB), f32),
            pltpu.VMEM((FB,), f32),
            pltpu.VMEM((FB,), f32),
            pltpu.VMEM((RB,), f32),
            dma((5,)),
        ],
        compiler_params=pltpu.CompilerParams(vmem_limit_bytes=30 * 2**20),
    )(u, rows, rn, bh, bl, col_moment)
    return w.T, rn, cn


def solution(mesh):
    in_specs = (P("col", "row"), P("row", "col"), P("row", None), P("row"), P("col"))
    out_specs = (P("row", "col"), P("row"), P("col"))
    return jax.shard_map(
        per_device, mesh=mesh, in_specs=in_specs, out_specs=out_specs, check_vma=False
    )
```

time: 69.1 us -> 53.7 us (0.78)
  local copies, waits for them, and re-layouts: 9.2 us -> 0.01 us
  Pallas kernels: 58.4 us -> 52.9 us
    unnamed x9 -> x2, local copies, waits for them, and re-layouts: 8.51 us -> 0.01 us
    pallas_call x1 -> x2, Pallas kernels: 58.4 us -> 52.9 us  [the longest x1 49.1 us: per_device(): pl.pallas_call(exchange, out_shape=(jax.ShapeDtypeStruct((2 * FH, R), f32...]
where the time goes in v2:
time: 53.7 us; the launch traced here: 53.6 us
  Pallas kernels  52.9 us (99%)
  between operations  0.66 us (1%)
    pallas_call x1, Pallas kernels, per_device(): pl.pallas_call(exchange, out_shape=(jax.ShapeDtypeStruct((2 * FH, R), f32...  49.1 us
    pallas_call x1, Pallas kernels, per_device(): pl.pallas_call(finish, out_shape=(jax.ShapeDtypeStruct((FB, DB), f32), ja...  3.75 us

profile of v2, /device:TPU:1, one launch (start us, length us, event | category | flops | bytes accessed | tf_op | source)
XLA Modules:
  0.0 53.6 jit_solution(11328930039941765202)
XLA Ops:
  0.6 0.0 copy-start
  0.6 49.1 %shard_map.76 = (f32[704,512]{1,0:T(8,128)S(1)}, f32[1,512]{1,0:T(1,128)S(1)}, f32[1,64]{1,0:T(1,128)S(1)}, bf16[512,1024]{1,0:T(8,128)(2,1)S(1)}, bf16[512,1024]{1,0:T(8,128)(2,1)S(1)}) custom-call(bf16[128,1024]{1,0:T(8,128)(2,1)} %act.1, bf16[688,512]{1,0:T(8,128)(2,1)} %bitcast.2, f32[1024,512]{1,0:T(8,128)} %basis.1, f32[64]{0:T(128)} %rm.1), custom_call_target="tpu_custom_call" | custom-call | tf_op jit(solution)/shard_map/pallas_call | solution.py:302
  49.8 0.0 copy-done
  49.8 3.7 %shard_map.77 = (f32[688,1024]{1,0:T(8,128)}, f32[64]{0:T(128)}, f32[688]{0:T(1024)}) custom-call(f32[704,512]{1,0:T(8,128)S(1)} %get-tuple-element.11.u, f32[1,512]{1,0:T(1,128)S(1)} %get-tuple-element.12.rows, f32[1,64]{1,0:T(1,128)S(1)} %get-tuple-element.13.rn, bf16[512,1024]{1,0:T(8,128)(2,1)S(1)} %get-tuple-element.14.bh, ...), custom_call_target="tpu_custom_call" | custom-call | tf_op jit(solution)/shard_map/pallas_call | solution.py:347
Async XLA Ops:
  0.6 49.2 %copy-start = (f32[688]{0:T(1024)S(1)}, f32[688]{0:T(1024)}, u32[]{:S(2)}) copy-start(f32[688]{0:T(1024)} %cm.1) | copy-start | bytes 8260

commit v3 on v2

v3 whole, which is shorter than its diff:
```python
import jax
import jax.numpy as jnp
from jax import lax
from jax.experimental import pallas as pl
from jax.experimental.pallas import tpu as pltpu
from jax.sharding import PartitionSpec as P

F = 22016
R = 512
MESH = pl.DeviceIdType.MESH
f32 = jnp.float32
bf16 = jnp.bfloat16

beta_two = 0.8
scale_alpha = 0.25
epsilon = 1e-30

NX, NY, NZ = 4, 4, 8
ROWS = 2 * NX
COLS = NY * NZ
RB = R // ROWS
RC = 2 * RB
TB = 128
TG = 512
DB = 1024
FB = F // COLS
FH = 352
FO = 2 * FH - FB
SB = RB // NY
LIFT = 2.0 ** 7.875


def split(v):
    high = v.astype(bf16)
    return high, (v - high.astype(f32)).astype(bf16)


def encode(u):
    top = jnp.maximum(jnp.max(jnp.abs(u), axis=0, keepdims=True), 1e-30)
    w = u * (LIFT / top)
    w = w * w
    w = w * w
    w = w * w
    w = w * w
    return jnp.where(u < 0, -w, w).astype(bf16), top * (1.0 / LIFT)


def decode(code, unit):
    t = code.astype(f32)
    m = jnp.exp2(jnp.log2(jnp.abs(t)) * 0.0625)
    m = jnp.where(t == 0, 0.0, m)
    return jnp.where(t < 0, -m, m) * unit


def exchange(act, grads, basis, rm, cm, u_out, rows_out, rn_out, cn_out, by_col_out, bh_out, bl_out,
             a_v, b_v, rm_v, cm_v, g_v, sp, su, srecv, urecv, frecv, furecv, senc, fenc, unit_own,
             sall, uall, fall, shl, shf, acc, fpenc, fpunit, fprecv, fpurecv,
             penc, punit, near_own, near_all, far_own, far_all,
             ld, s1s, s1r, u1s, u1r, f1s, f1r, fu1s, fu1r, bds, bdr, fds, fdr, fws, uzs, uzr, uys, uyr,
             g1s, g2s, g1r, g2r, gss, gsr, sss, ssr, fss, fsr, fps, fpr,
             pds, pdr, pus, pur, sps, spr, sus, sur, nes, ner, fas, far, ysem):
    row, col = lax.axis_index("row"), lax.axis_index("col")
    x, k = row // 2, row % 2
    y, z = col // NZ, col % NZ

    def at_x(o, core):
        return (lax.rem(x + o + NX, NX) * 2 + core, col)

    sibling = (x * 2 + 1 - k, col)
    opposite = lax.rem(x + 2, NX)
    here = y != opposite

    def send(src, dst, ssem, rsem, dev):
        pltpu.make_async_remote_copy(src_ref=src, dst_ref=dst, send_sem=ssem, recv_sem=rsem,
                                     device_id=dev, device_id_type=MESH).start()

    def arrived(ref, sem):
        pltpu.make_async_copy(ref, ref, sem).wait()

    def half(core):
        return grads.at[pl.ds(core * (FB - FH), FH)]

    loads = [
        pltpu.make_async_copy(basis, b_v, ld.at[0]),
        pltpu.make_async_copy(act, a_v, ld.at[1]),
        pltpu.make_async_copy(half(k), g_v.at[row], ld.at[2]),
        pltpu.make_async_copy(rm, rm_v, ld.at[3]),
        pltpu.make_async_copy(cm, cm_v, ld.at[4]),
    ]
    for load in loads:
        load.start()

    barrier = pltpu.get_barrier_semaphore()
    for i in range(1, ROWS):
        pl.semaphore_signal(barrier, inc=1, device_id=(lax.rem(row + i, ROWS), col), device_id_type=MESH)
    for i in range(1, NZ):
        pl.semaphore_signal(barrier, inc=1, device_id=(row, y * NZ + lax.rem(z + i, NZ)), device_id_type=MESH)
    for i in range(1, NY):
        pl.semaphore_signal(barrier, inc=1, device_id=(row, lax.rem(y + i, NY) * NZ + z), device_id_type=MESH)
    @pl.when(y != x)
    def _():
        for r in range(ROWS):
            pl.semaphore_signal(barrier, inc=1, device_id=(r, x * NZ + z), device_id_type=MESH)
    pl.semaphore_wait(barrier, ROWS + NZ + NY - 3 + 2 * (NY - 1))

    for i in range(1, NY):
        pl.semaphore_signal(ysem, inc=1, device_id=(row, lax.rem(y + i, NY) * NZ + z), device_id_type=MESH)

    loads[0].wait()
    loads[1].wait()
    b_h, b_l = split(b_v[...])
    a = a_v[...]
    part = jnp.dot(a, b_h, preferred_element_type=f32) + jnp.dot(a, b_l, preferred_element_type=f32)
    part = part.T
    for r in range(ROWS):
        code, unit = encode(part[r * RB:(r + 1) * RB])
        sp[r] = code
        su[r] = unit
    for i in range(1, ROWS):
        peer = lax.rem(row + i, ROWS)

        @pl.when(peer // 2 != lax.rem(y + 2, NY))
        def _():
            send(sp.at[peer], srecv.at[row], s1s.at[i], s1r.at[i], (peer, col))
            send(su.at[peer], urecv.at[row], u1s.at[i], u1r.at[i], (peer, col))
    over = lax.rem(y + 2, NY) * 2
    for core in range(2):
        for j in range(NY):
            @pl.when((y * 2 + core != row) | (y != j))
            def _():
                dev = (y * 2 + core, j * NZ + z)
                send(sp.at[over + core, pl.ds(j * SB, SB)], frecv.at[row], f1s.at[core * NY + j], f1r.at[row], dev)
                send(su.at[over + core], furecv.at[row], fu1s.at[core * NY + j], fu1r.at[row], dev)
    for core in range(2):
        send(half(core), g_v.at[row], g1s.at[core], g1r.at[k], at_x(1, core))
        send(half(core), g_v.at[row], g2s.at[core], g2r.at[k], at_x(-1, core))
    send(half(1 - k), g_v.at[row], gss, gsr, sibling)
    for load in loads[2:]:
        load.wait()

    pl.semaphore_wait(ysem, NY - 1)

    @pl.when(y == x)
    def _():
        frecv[row] = sp[opposite * 2 + k, pl.ds(pl.multiple_of(y * SB, SB), SB)]
        furecv[row] = su[opposite * 2 + k]
    for r in range(ROWS):
        @pl.when((y != x) | (row != r))
        def _():
            arrived(frecv.at[row], f1r.at[r])
            arrived(furecv.at[row], fu1r.at[r])
    total = decode(frecv[0], furecv[0])
    for r in range(1, ROWS):
        total = total + decode(frecv[r], furecv[r])
    code, unit = encode(total)
    fenc[...] = code
    unit_own[1] = unit
    fall[k, z, pl.ds(pl.multiple_of(y * SB, SB), SB)] = code
    unit_own[0] = unit

    @pl.when(here)
    def _():
        srecv[row] = sp[row]
        urecv[row] = su[row]
        for i in range(1, ROWS):
            arrived(srecv.at[row], s1r.at[i])
            arrived(urecv.at[row], u1r.at[i])
        total = decode(srecv[0], urecv[0])
        for r in range(1, ROWS):
            total = total + decode(srecv[r], urecv[r])
        code, unit = encode(total)
        senc[...] = code
        unit_own[0] = unit
        sall[k, col] = code
    uall[k, y, z] = unit_own[...]
    for j in range(1, NZ):
        send(unit_own, uall.at[k, y, z], uzs.at[j], uzr.at[j], (row, y * NZ + lax.rem(z + j, NZ)))

    for d in (1, 2, 3, 0):
        @pl.loop(0 if d else 1, NZ)
        def _(j):
            dev = (row, lax.rem(y + d, NY) * NZ + lax.rem(z + j, NZ))
            send(fenc, fall.at[k, z, pl.ds(pl.multiple_of(y * SB, SB), SB)], fds.at[d * NZ + j], fdr.at[d * NZ + j], dev)

    @pl.when(here)
    def _():
        for j in (2, 6, 1, 7, 0):
            for d in (1, 2, 3, 0):
                if j or d:
                    dev = (row, lax.rem(y + d, NY) * NZ + lax.rem(z + j, NZ))
                    send(senc, sall.at[k, col], bds.at[d * NZ + j], bdr.at[d * NZ + j], dev)

    before = lax.rem(x + NX - 1, NX) * 2
    after = lax.rem(x + 1, NX) * 2
    turned_h, turned_l = split(b_v[...].T)
    bh_out[...] = turned_h
    bl_out[...] = turned_l

    def project(g, sides):
        return lax.dot_general(g, sides, (((1,), (1,)), ((), ())), preferred_element_type=f32)

    for j in range(1, NZ):
        arrived(unit_own, uzr.at[j])
    for d in range(1, NY):
        send(uall.at[k, y], uall.at[k, y], uys.at[d], uyr.at[d], (row, lax.rem(y + d, NY) * NZ + z))

    def hand_on(d, source, j, sem):
        b = lax.rem(y + NY - d, NY) * NZ + lax.rem(z + source, NZ)
        dev = (row, y * NZ + lax.rem(z + j, NZ))
        send(sall.at[k, b], sall.at[k, b], fws.at[d * 4 + sem], bdr.at[d * NZ + lax.rem(NZ - source + j, NZ)], dev)

    for d in (1, 2, 3, 0):
        @pl.when(lax.rem(y + NY - d, NY) != opposite)
        def _():
            arrived(senc, bdr.at[d * NZ + 2])
            hand_on(d, NZ - 2, 1, 0)
            arrived(senc, bdr.at[d * NZ + 6])
            hand_on(d, 2, NZ - 1, 1)

            @pl.when(z % 2 == 0)
            def _():
                hand_on(d, NZ - 2, 2, 2)

            @pl.when(z % 2 == 1)
            def _():
                hand_on(d, 2, NZ - 2, 2)

    for d in (1, 2, 3, 0):
        @pl.loop(0 if d else 1, NZ)
        def _(j):
            arrived(fenc, fdr.at[d * NZ + j])
    send(fall.at[k], fall.at[k], fss.at[0], fsr.at[0], sibling)
    for d in range(1, NY):
        arrived(uall.at[k, y], uyr.at[d])
    send(uall.at[k], uall.at[k], fss.at[1], fsr.at[1], sibling)
    arrived(g_v.at[row], gsr)
    arrived(fall.at[k], fsr.at[0])
    arrived(uall.at[k], fsr.at[1])
    for b in range(NZ):
        r, at = b // 4, b % 4 * TB
        for core in range(2):
            units = jnp.concatenate([jnp.broadcast_to(uall[core, j, b, 1], (SB, TB)) for j in range(NY)], axis=0)
            high, low = split(decode(fall[core, b], units))
            shf[r, core * RB:(core + 1) * RB, at:at + TB] = high
            shf[r, RC + core * RB:RC + (core + 1) * RB, at:at + TB] = low
    acc[...] = project(g_v[x * 2], shf[0])
    acc[...] += project(g_v[x * 2 + 1], shf[1])
    code, unit = encode(acc[:, 0:RC] + acc[:, RC:2 * RC])
    fpenc[...] = code
    fpunit[...] = unit
    send(fpenc, fprecv, fps.at[0], fpr.at[0], at_x(2, k))
    send(fpunit, fpurecv, fps.at[1], fpr.at[1], at_x(2, k))

    def share(d):
        first = lax.rem(y + NY - d, NY)

        @pl.when(first != opposite)
        def _():
            for j in (0, 1, 7, 3, 4, 5):
                if j or d:
                    arrived(senc, bdr.at[d * NZ + j])
            some = pl.ds(first * NZ, NZ)
            send(sall.at[k, some], sall.at[k, some], sss.at[d], ssr.at[d], sibling)

    def unpack(d):
        first = lax.rem(y + NY - d, NY)

        @pl.when(first != opposite)
        def _():
            some = pl.ds(first * NZ, NZ)
            arrived(sall.at[k, some], ssr.at[d])
            for j in range(NZ):
                b = first * NZ + j
                r = first * 2 + j // 4
                at = j % 4 * TB
                for core in range(2):
                    high, low = split(decode(sall[core, b], uall[core, first, j, 0]))
                    shl[r, core * RB:(core + 1) * RB, at:at + TB] = high
                    shl[r, RC + core * RB:RC + (core + 1) * RB, at:at + TB] = low

    share(1)
    share(2)
    unpack(1)
    share(3)
    unpack(2)
    share(0)
    unpack(3)
    unpack(0)

    acc[...] = project(g_v[x * 2], shl[x * 2])
    acc[...] += project(g_v[x * 2 + 1], shl[x * 2 + 1])
    for i in range(2):
        arrived(g_v.at[row], g1r.at[i])
        acc[...] += project(g_v[before + i], shl[before + i])
    for i in range(2):
        arrived(g_v.at[row], g2r.at[i])
        acc[...] += project(g_v[after + i], shl[after + i])
    arrived(fprecv, fpr.at[0])
    arrived(fpurecv, fpr.at[1])

    mine = acc[:, 0:RC] + acc[:, RC:2 * RC] + decode(fprecv[...], fpurecv[...])
    own = lax.broadcasted_iota(jnp.int32, (FH, RC), 0) >= FO * k
    sums = jnp.sum(jnp.where(own, mine * mine + epsilon, 0.0), axis=0, keepdims=True)
    old = rm_v[...].reshape(1, RB)
    old = jnp.concatenate([old, old], axis=1)
    lane = lax.broadcasted_iota(jnp.int32, (1, RC), 1)
    joins = (lane // RB == k) & (col == 0)
    near = (1.0 - beta_two) * (sums / F) + jnp.where(joins, beta_two * old, 0.0)
    near_own[...] = near
    near_at = k * NZ + z
    near_all[near_at] = near

    @pl.loop(1, 2 * NZ)
    def _(i):
        to = lax.rem(near_at + i, 2 * NZ)
        send(near_own, near_all.at[near_at], nes.at[i], ner.at[i], (x * 2 + to // NZ, y * NZ + lax.rem(to, NZ)))

    code, unit = encode(mine)
    penc[row] = code
    punit[row] = unit
    for i in (2, 1, 3):
        send(penc.at[row], penc.at[row], pds.at[i], pdr.at[i], at_x(i, k))
        send(punit.at[row], punit.at[row], pus.at[i], pur.at[i], at_x(i, k))
    send(penc.at[row], penc.at[row], sps.at[0], spr.at[0], sibling)
    send(punit.at[row], punit.at[row], sus.at[0], sur.at[0], sibling)

    @pl.loop(1, 2 * NZ)
    def _(i):
        arrived(near_own, ner.at[i])

    mid = jnp.sum(near_all[...], axis=0)
    far_own[...] = mid
    far_at = y * NX + x
    far_all[far_at] = mid

    @pl.loop(1, NX * NY)
    def _(i):
        to = lax.rem(far_at + i, NX * NY)
        send(far_own, far_all.at[far_at], fas.at[i], far.at[i], (lax.rem(to, NX) * 2 + k, to // NX * NZ + z))

    for i in (1, 3, 2):
        piece = lax.rem(x + NX - i, NX) * 2 + k
        arrived(penc.at[piece], pdr.at[i])
        send(penc.at[piece], penc.at[piece], sps.at[i], spr.at[i], sibling)
        arrived(punit.at[piece], pur.at[i])
        send(punit.at[piece], punit.at[piece], sus.at[i], sur.at[i], sibling)
    for i in range(NX):
        arrived(penc.at[row], spr.at[i])
        arrived(punit.at[row], sur.at[i])
    col_sum = [jnp.zeros((FH, 1), f32), jnp.zeros((FB - FH, 1), f32)]
    for r in range(ROWS):
        c = r % 2
        u = decode(penc[r], punit[r])[FO * c:]
        u_out[c * FH:c * FH + FH - FO * c, (r // 2) * RC:(r // 2 + 1) * RC] = u
        col_sum[c] += jnp.sum(u * u + epsilon, axis=1, keepdims=True)
    old = jnp.broadcast_to(cm_v[...].reshape(1, FB), (128, FB)).T
    col_next = beta_two * old + (1.0 - beta_two) * (jnp.concatenate(col_sum, axis=0) / R)
    cn_out[...] = col_next.T[0]
    by_col_out[...] = 1.0 / jnp.sqrt(col_next)

    for i in range(1, ROWS):
        @pl.when(lax.rem(row + i, ROWS) // 2 != lax.rem(y + 2, NY))
        def _():
            arrived(srecv.at[row], s1s.at[i])
            arrived(urecv.at[row], u1s.at[i])
    for core in range(2):
        for j in range(NY):
            @pl.when((y * 2 + core != row) | (y != j))
            def _():
                arrived(frecv.at[row], f1s.at[core * NY + j])
                arrived(furecv.at[row], fu1s.at[core * NY + j])

    @pl.loop(1, COLS)
    def _(i):
        arrived(fenc, fds.at[i])

    @pl.when(here)
    def _():
        for d in range(NY):
            for j in (0, 1, 2, 6, 7):
                if j or d:
                    arrived(senc, bds.at[d * NZ + j])
    for j in range(1, NZ):
        arrived(unit_own, uzs.at[j])
    for d in range(1, NY):
        arrived(uall.at[k, y], uys.at[d])

    @pl.loop(1, 2 * NZ)
    def _(i):
        arrived(near_own, nes.at[i])
    for i in range(2):
        arrived(g_v.at[row], g1s.at[i])
        arrived(g_v.at[row], g2s.at[i])
    arrived(g_v.at[row], gss)
    arrived(fall.at[k], fss.at[0])
    arrived(uall.at[k], fss.at[1])
    arrived(fpenc, fps.at[0])
    arrived(fpunit, fps.at[1])
    for d in range(NY):
        @pl.when(lax.rem(y + NY - d, NY) != opposite)
        def _():
            arrived(sall.at[k, pl.ds(0, NZ)], sss.at[d])
            for i in range(3):
                arrived(senc, fws.at[d * 4 + i])

    @pl.loop(1, NX * NY)
    def _(i):
        arrived(far_own, far.at[i])
        arrived(far_own, fas.at[i])

    for i in range(NX):
        rows = far_all[i]
        for j in range(1, NY):
            rows = rows + far_all[j * NX + i]
        rows_out[:, i * RC:(i + 1) * RC] = rows
    rows = far_all[x]
    for j in range(1, NY):
        rows = rows + far_all[j * NX + x]
    rn_out[...] = jnp.where(k == 0, rows[:, 0:RB], rows[:, RB:RC]).reshape(RB)

    for i in range(NX):
        arrived(penc.at[row], sps.at[i])
        arrived(punit.at[row], sus.at[i])
    for i in range(1, NX):
        arrived(penc.at[row], pds.at[i])
        arrived(punit.at[row], pus.at[i])


NT = 256


def finish(u, rows, rn, cn, by_col, bh, bl, w_out, rn_out, cn_out, v_h, v_l, w_v, sem):
    puts = [pltpu.make_async_copy(rn, rn_out, sem.at[0]), pltpu.make_async_copy(cn, cn_out, sem.at[1])]
    for put in puts:
        put.start()
    by_row = 1.0 / jnp.sqrt(rows[...])
    row_mean = jnp.sum(rows[...], axis=1, keepdims=True) / R
    top = scale_alpha * jnp.sqrt(row_mean)
    v_h[...], v_l[...] = split(u[...] * by_row)
    by = by_col[:, 0:1] * top
    for n in range(DB // NT):
        cols = pl.ds(n * NT, NT)
        w = jnp.dot(v_h[...], bh[:, n * NT:(n + 1) * NT], preferred_element_type=f32)
        w += jnp.dot(v_l[...], bh[:, n * NT:(n + 1) * NT], preferred_element_type=f32)
        w += jnp.dot(v_h[...], bl[:, n * NT:(n + 1) * NT], preferred_element_type=f32)
        w_v[:, n * NT:(n + 1) * NT] = w * by
        put = pltpu.make_async_copy(w_v.at[:, cols], w_out.at[:, cols], sem.at[2 + n])
        put.start()
        puts.append(put)
    for put in puts:
        put.wait()


def per_device(activations, out_grads, basis, row_moment, col_moment):
    hbm = pl.BlockSpec(memory_space=pltpu.HBM)
    vmem = pl.BlockSpec(memory_space=pltpu.VMEM)
    dma = pltpu.SemaphoreType.DMA
    u, rows, rn, cn, by_col, bh, bl = pl.pallas_call(
        exchange,
        out_shape=(
            jax.ShapeDtypeStruct((FB, R), f32),
            jax.ShapeDtypeStruct((1, R), f32),
            jax.ShapeDtypeStruct((RB,), f32),
            jax.ShapeDtypeStruct((FB,), f32),
            jax.ShapeDtypeStruct((FB, 128), f32),
            jax.ShapeDtypeStruct((R, DB), bf16),
            jax.ShapeDtypeStruct((R, DB), bf16),
        ),
        in_specs=[hbm] * 5,
        out_specs=(vmem,) * 7,
        scratch_shapes=[
            pltpu.VMEM((TB, DB), bf16),
            pltpu.VMEM((DB, R), f32),
            pltpu.VMEM((RB,), f32),
            pltpu.VMEM((FB,), f32),
            pltpu.VMEM((ROWS, FH, TG), bf16),
            pltpu.VMEM((ROWS, RB, TB), bf16),
            pltpu.VMEM((ROWS, 1, TB), f32),
            pltpu.VMEM((ROWS, RB, TB), bf16),
            pltpu.VMEM((ROWS, 1, TB), f32),
            pltpu.VMEM((ROWS, SB, TB), bf16),
            pltpu.VMEM((ROWS, 1, TB), f32),
            pltpu.VMEM((RB, TB), bf16),
            pltpu.VMEM((SB, TB), bf16),
            pltpu.VMEM((2, 1, TB), f32),
            pltpu.VMEM((2, COLS, RB, TB), bf16),
            pltpu.VMEM((2, NY, NZ, 2, 1, TB), f32),
            pltpu.VMEM((2, NZ, RB, TB), bf16),
            pltpu.VMEM((ROWS, 2 * RC, TG), bf16),
            pltpu.VMEM((2, 2 * RC, TG), bf16),
            pltpu.VMEM((FH, 2 * RC), f32),
            pltpu.VMEM((FH, RC), bf16),
            pltpu.VMEM((1, RC), f32),
            pltpu.VMEM((FH, RC), bf16),
            pltpu.VMEM((1, RC), f32),
            pltpu.VMEM((ROWS, FH, RC), bf16),
            pltpu.VMEM((ROWS, 1, RC), f32),
            pltpu.VMEM((1, RC), f32),
            pltpu.VMEM((2 * NZ, 1, RC), f32),
            pltpu.VMEM((1, RC), f32),
            pltpu.VMEM((NX * NY, 1, RC), f32),
            dma((5,)),
            *[dma((ROWS,))] * 8,
            *[dma((COLS,))] * 4,
            dma((4 * NY,)), dma((NZ,)), dma((NZ,)), dma((NY,)), dma((NY,)),
            dma((2,)), dma((2,)), dma((2,)), dma((2,)), dma, dma,
            dma((NY,)), dma((NY,)),
            dma((2,)), dma((2,)), dma((2,)), dma((2,)),
            dma((NX,)), dma((NX,)), dma((NX,)), dma((NX,)),
            dma((NX,)), dma((NX,)), dma((NX,)), dma((NX,)),
            dma((2 * NZ,)), dma((2 * NZ,)),
            dma((NX * NY,)), dma((NX * NY,)),
            pltpu.SemaphoreType.REGULAR,
        ],
        compiler_params=pltpu.CompilerParams(
            collective_id=0, has_side_effects=True, vmem_limit_bytes=30 * 2**20
        ),
    )(*[pltpu.with_memory_space_constraint(v, pltpu.HBM) for v in (activations, out_grads.T, basis, row_moment, col_moment)])
    w, rn, cn = pl.pallas_call(
        finish,
        out_shape=(
            jax.ShapeDtypeStruct((FB, DB), f32),
            jax.ShapeDtypeStruct((RB,), f32),
            jax.ShapeDtypeStruct((FB,), f32),
        ),
        in_specs=[vmem] * 7,
        out_specs=(hbm,) * 3,
        scratch_shapes=[
            pltpu.VMEM((FB, R), bf16),
            pltpu.VMEM((FB, R), bf16),
            pltpu.VMEM((FB, DB), f32),
            dma((2 + DB // NT,)),
        ],
        compiler_params=pltpu.CompilerParams(vmem_limit_bytes=30 * 2**20),
    )(u, rows, rn, cn, by_col, bh, bl)
    return w.T, rn, cn


def solution(mesh):
    in_specs = (P("col", "row"), P("row", "col"), P("row", None), P("row"), P("col"))
    out_specs = (P("row", "col"), P("row"), P("col"))
    return jax.shard_map(
        per_device, mesh=mesh, in_specs=in_specs, out_specs=out_specs, check_vma=False
    )
```

time: 53.7 us -> 51.4 us (0.957)
  Pallas kernels: 52.9 us -> 50.7 us
    pallas_call x1, Pallas kernels: 49.1 us -> 47.1 us  [per_device(): pl.pallas_call(exchange, out_shape=(jax.ShapeDtypeStruct((FB, R), f32), j...]
where the time goes in v3:
time: 51.4 us
  Pallas kernels  50.7 us (99%)
  between operations  0.64 us (1%)
    pallas_call x1, Pallas kernels, per_device(): pl.pallas_call(exchange, out_shape=(jax.ShapeDtypeStruct((FB, R), f32), j...  47.1 us
    pallas_call x1, Pallas kernels, per_device(): pl.pallas_call(finish, out_shape=(jax.ShapeDtypeStruct((FB, DB), f32), ja...  3.63 us

profile of v3, /device:TPU:1, one launch (start us, length us, event | category | flops | bytes accessed | tf_op | source)
XLA Modules:
  0.0 51.4 jit_solution(16089493911292919061)
XLA Ops:
  0.6 47.1 %shard_map.76 = (f32[688,512]{1,0:T(8,128)S(1)}, f32[1,512]{1,0:T(1,128)S(1)}, f32[64]{0:T(128)S(1)}, f32[688]{0:T(1024)S(1)}, f32[688,128]{1,0:T(8,128)S(1)}, /...) custom-call(bf16[128,1024]{1,0:T(8,128)(2,1)} %act.1, bf16[688,512]{1,0:T(8,128)(2,1)} %bitcast.2, ...), custom_call_target="tpu_custom_call" | custom-call | tf_op jit(solution)/shard_map/pallas_call | solution.py:458
  47.7 3.6 %shard_map.77 = (f32[688,1024]{1,0:T(8,128)}, f32[64]{0:T(128)}, f32[688]{0:T(1024)}) custom-call(f32[688,512]{1,0:T(8,128)S(1)} %get-tuple-element.13.u, f32[1,512]{1,0:T(1,128)S(1)} %get-tuple-element.14.rows, f32[64]{0:T(128)S(1)} %get-tuple-element.15.rn, f32[688]{0:T(1024)S(1)} %get-tuple-element.16.cn, f32[688,128]{1,0:T(8,128)S(1)} %get-tuple-element.17.by_col, ...), custom_call_target="tpu_custom_call" | custom-call | tf_op jit(solution)/shard_map/pallas_call | solution.py:519

commit v4 on v3

--- a/solution.py
+++ b/solution.py
@@ -57,7 +57,7 @@
              sall, uall, fall, shl, shf, acc, fpenc, fpunit, fprecv, fpurecv,
              penc, punit, near_own, near_all, far_own, far_all,
              ld, s1s, s1r, u1s, u1r, f1s, f1r, fu1s, fu1r, bds, bdr, fds, fdr, fws, uzs, uzr, uys, uyr,
-             g1s, g2s, g1r, g2r, gss, gsr, sss, ssr, fss, fsr, fps, fpr,
+             g1s, g2s, gr, gss, sss, ssr, fss, fsr, fps, fpr,
              pds, pdr, pus, pur, sps, spr, sus, sur, nes, ner, fas, far, ysem):
     row, col = lax.axis_index("row"), lax.axis_index("col")
     x, k = row // 2, row % 2
@@ -80,14 +80,18 @@
     def half(core):
         return grads.at[pl.ds(core * (FB - FH), FH)]
 
+    DH = DB // 2
+    first = [
+        pltpu.make_async_copy(act, a_v, ld.at[0]),
+        pltpu.make_async_copy(basis.at[pl.ds(0, DH)], b_v.at[pl.ds(0, DH)], ld.at[1]),
+        pltpu.make_async_copy(basis.at[pl.ds(DH, DH)], b_v.at[pl.ds(DH, DH)], ld.at[2]),
+    ]
     loads = [
-        pltpu.make_async_copy(basis, b_v, ld.at[0]),
-        pltpu.make_async_copy(act, a_v, ld.at[1]),
-        pltpu.make_async_copy(half(k), g_v.at[row], ld.at[2]),
-        pltpu.make_async_copy(rm, rm_v, ld.at[3]),
-        pltpu.make_async_copy(cm, cm_v, ld.at[4]),
+        pltpu.make_async_copy(half(k), g_v.at[row], ld.at[3]),
+        pltpu.make_async_copy(rm, rm_v, ld.at[4]),
+        pltpu.make_async_copy(cm, cm_v, ld.at[5]),
     ]
-    for load in loads:
+    for load in first:
         load.start()
 
     barrier = pltpu.get_barrier_semaphore()
@@ -101,21 +105,22 @@
     def _():
         for r in range(ROWS):
             pl.semaphore_signal(barrier, inc=1, device_id=(r, x * NZ + z), device_id_type=MESH)
-    pl.semaphore_wait(barrier, ROWS + NZ + NY - 3 + 2 * (NY - 1))
-
-    for i in range(1, NY):
-        pl.semaphore_signal(ysem, inc=1, device_id=(row, lax.rem(y + i, NY) * NZ + z), device_id_type=MESH)
-
-    loads[0].wait()
-    loads[1].wait()
-    b_h, b_l = split(b_v[...])
-    a = a_v[...]
-    part = jnp.dot(a, b_h, preferred_element_type=f32) + jnp.dot(a, b_l, preferred_element_type=f32)
+
+    first[0].wait()
+    part = jnp.zeros((TB, R), f32)
+    for h in range(2):
+        first[1 + h].wait()
+        high, low = split(b_v[h * DH:(h + 1) * DH, :])
+        a = a_v[:, h * DH:(h + 1) * DH]
+        part = part + jnp.dot(a, high, preferred_element_type=f32) + jnp.dot(a, low, preferred_element_type=f32)
     part = part.T
     for r in range(ROWS):
         code, unit = encode(part[r * RB:(r + 1) * RB])
         sp[r] = code
         su[r] = unit
+    pl.semaphore_wait(barrier, ROWS + NZ + NY - 3 + 2 * (NY - 1))
+    for i in range(1, NY):
+        pl.semaphore_signal(ysem, inc=1, device_id=(row, lax.rem(y + i, NY) * NZ + z), device_id_type=MESH)
     for i in range(1, ROWS):
         peer = lax.rem(row + i, ROWS)
 
@@ -131,14 +136,15 @@
                 dev = (y * 2 + core, j * NZ + z)
                 send(sp.at[over + core, pl.ds(j * SB, SB)], frecv.at[row], f1s.at[core * NY + j], f1r.at[row], dev)
                 send(su.at[over + core], furecv.at[row], fu1s.at[core * NY + j], fu1r.at[row], dev)
+    for load in loads:
+        load.start()
+
+    pl.semaphore_wait(ysem, NY - 1)
+
     for core in range(2):
-        send(half(core), g_v.at[row], g1s.at[core], g1r.at[k], at_x(1, core))
-        send(half(core), g_v.at[row], g2s.at[core], g2r.at[k], at_x(-1, core))
-    send(half(1 - k), g_v.at[row], gss, gsr, sibling)
-    for load in loads[2:]:
-        load.wait()
-
-    pl.semaphore_wait(ysem, NY - 1)
+        send(half(core), g_v.at[row], g1s.at[core], gr.at[row], at_x(1, core))
+        send(half(core), g_v.at[row], g2s.at[core], gr.at[row], at_x(-1, core))
+    send(half(1 - k), g_v.at[row], gss, gr.at[row], sibling)
 
     @pl.when(y == x)
     def _():
@@ -176,22 +182,23 @@
     for j in range(1, NZ):
         send(unit_own, uall.at[k, y, z], uzs.at[j], uzr.at[j], (row, y * NZ + lax.rem(z + j, NZ)))
 
+    def spread(steps):
+        @pl.when(here)
+        def _():
+            for j in steps:
+                for d in (1, 2, 3, 0):
+                    if j or d:
+                        dev = (row, lax.rem(y + d, NY) * NZ + lax.rem(z + j, NZ))
+                        send(senc, sall.at[k, col], bds.at[d * NZ + j], bdr.at[d * NZ + j], dev)
+
+    spread((2, 6))
     for d in (1, 2, 3, 0):
         @pl.loop(0 if d else 1, NZ)
         def _(j):
             dev = (row, lax.rem(y + d, NY) * NZ + lax.rem(z + j, NZ))
             send(fenc, fall.at[k, z, pl.ds(pl.multiple_of(y * SB, SB), SB)], fds.at[d * NZ + j], fdr.at[d * NZ + j], dev)
-
-    @pl.when(here)
-    def _():
-        for j in (2, 6, 1, 7, 0):
-            for d in (1, 2, 3, 0):
-                if j or d:
-                    dev = (row, lax.rem(y + d, NY) * NZ + lax.rem(z + j, NZ))
-                    send(senc, sall.at[k, col], bds.at[d * NZ + j], bdr.at[d * NZ + j], dev)
-
-    before = lax.rem(x + NX - 1, NX) * 2
-    after = lax.rem(x + 1, NX) * 2
+    spread((1, 7, 0))
+
     turned_h, turned_l = split(b_v[...].T)
     bh_out[...] = turned_h
     bl_out[...] = turned_l
@@ -233,7 +240,7 @@
     for d in range(1, NY):
         arrived(uall.at[k, y], uyr.at[d])
     send(uall.at[k], uall.at[k], fss.at[1], fsr.at[1], sibling)
-    arrived(g_v.at[row], gsr)
+    arrived(g_v.at[row], gr.at[x * 2 + 1 - k])
     arrived(fall.at[k], fsr.at[0])
     arrived(uall.at[k], fsr.at[1])
     for b in range(NZ):
@@ -243,6 +250,8 @@
             high, low = split(decode(fall[core, b], units))
             shf[r, core * RB:(core + 1) * RB, at:at + TB] = high
             shf[r, RC + core * RB:RC + (core + 1) * RB, at:at + TB] = low
+    for load in loads:
+        load.wait()
     acc[...] = project(g_v[x * 2], shf[0])
     acc[...] += project(g_v[x * 2 + 1], shf[1])
     code, unit = encode(acc[:, 0:RC] + acc[:, RC:2 * RC])
@@ -278,23 +287,31 @@
                     shl[r, core * RB:(core + 1) * RB, at:at + TB] = high
                     shl[r, RC + core * RB:RC + (core + 1) * RB, at:at + TB] = low
 
+    def add(d):
+        first = lax.rem(y + NY - d, NY)
+
+        @pl.when(first != opposite)
+        def _():
+            @pl.when(first != x)
+            def _():
+                arrived(g_v.at[row], gr.at[first * 2])
+                arrived(g_v.at[row], gr.at[first * 2 + 1])
+            for i in range(2):
+                acc[...] += project(g_v[first * 2 + i], shl[first * 2 + i])
+
+    acc[...] = jnp.zeros_like(acc)
     share(1)
     share(2)
     unpack(1)
     share(3)
     unpack(2)
+    add(1)
     share(0)
     unpack(3)
+    add(2)
     unpack(0)
-
-    acc[...] = project(g_v[x * 2], shl[x * 2])
-    acc[...] += project(g_v[x * 2 + 1], shl[x * 2 + 1])
-    for i in range(2):
-        arrived(g_v.at[row], g1r.at[i])
-        acc[...] += project(g_v[before + i], shl[before + i])
-    for i in range(2):
-        arrived(g_v.at[row], g2r.at[i])
-        acc[...] += project(g_v[after + i], shl[after + i])
+    add(3)
+    add(0)
     arrived(fprecv, fpr.at[0])
     arrived(fpurecv, fpr.at[1])
 
@@ -499,11 +516,11 @@
             pltpu.VMEM((2 * NZ, 1, RC), f32),
             pltpu.VMEM((1, RC), f32),
             pltpu.VMEM((NX * NY, 1, RC), f32),
-            dma((5,)),
+            dma((6,)),
             *[dma((ROWS,))] * 8,
             *[dma((COLS,))] * 4,
             dma((4 * NY,)), dma((NZ,)), dma((NZ,)), dma((NY,)), dma((NY,)),
-            dma((2,)), dma((2,)), dma((2,)), dma((2,)), dma, dma,
+            dma((2,)), dma((2,)), dma((ROWS,)), dma,
             dma((NY,)), dma((NY,)),
             dma((2,)), dma((2,)), dma((2,)), dma((2,)),
             dma((NX,)), dma((NX,)), dma((NX,)), dma((NX,)),

time: 51.4 us -> 51.1 us (level)
  no operation moved by 1% of the time
where the time goes in v4:
time: 51.1 us; the launch traced here: 51 us
  Pallas kernels  50.3 us (98%)
  between operations  0.64 us (1%)
    pallas_call x1, Pallas kernels, per_device(): pl.pallas_call(exchange, out_shape=(jax.ShapeDtypeStruct((FB, R), f32), j...  46.7 us
    pallas_call x1, Pallas kernels, per_device(): pl.pallas_call(finish, out_shape=(jax.ShapeDtypeStruct((FB, DB), f32), ja...  3.63 us

profile of v4, /device:TPU:1, one launch (start us, length us, event | category | flops | bytes accessed | tf_op | source)
XLA Modules:
  0.0 51.0 jit_solution(8035527442908859945)
XLA Ops:
  0.6 46.7 %shard_map.76 = (f32[688,512]{1,0:T(8,128)S(1)}, f32[1,512]{1,0:T(1,128)S(1)}, f32[64]{0:T(128)S(1)}, f32[688]{0:T(1024)S(1)}, f32[688,128]{1,0:T(8,128)S(1)}, /...) custom-call(bf16[128,1024]{1,0:T(8,128)(2,1)} %act.1, bf16[688,512]{1,0:T(8,128)(2,1)} %bitcast.2, ...), custom_call_target="tpu_custom_call" | custom-call | tf_op jit(solution)/shard_map/pallas_call | solution.py:475
  47.3 3.6 %shard_map.77 = (f32[688,1024]{1,0:T(8,128)}, f32[64]{0:T(128)}, f32[688]{0:T(1024)}) custom-call(f32[688,512]{1,0:T(8,128)S(1)} %get-tuple-element.13.u, f32[1,512]{1,0:T(1,128)S(1)} %get-tuple-element.14.rows, f32[64]{0:T(128)S(1)} %get-tuple-element.15.rn, f32[688]{0:T(1024)S(1)} %get-tuple-element.16.cn, f32[688,128]{1,0:T(8,128)S(1)} %get-tuple-element.17.by_col, ...), custom_call_target="tpu_custom_call" | custom-call | tf_op jit(solution)/shard_map/pallas_call | solution.py:536

commit v5 on v4

--- a/solution.py
+++ b/solution.py
@@ -121,13 +121,6 @@
     pl.semaphore_wait(barrier, ROWS + NZ + NY - 3 + 2 * (NY - 1))
     for i in range(1, NY):
         pl.semaphore_signal(ysem, inc=1, device_id=(row, lax.rem(y + i, NY) * NZ + z), device_id_type=MESH)
-    for i in range(1, ROWS):
-        peer = lax.rem(row + i, ROWS)
-
-        @pl.when(peer // 2 != lax.rem(y + 2, NY))
-        def _():
-            send(sp.at[peer], srecv.at[row], s1s.at[i], s1r.at[i], (peer, col))
-            send(su.at[peer], urecv.at[row], u1s.at[i], u1r.at[i], (peer, col))
     over = lax.rem(y + 2, NY) * 2
     for core in range(2):
         for j in range(NY):
@@ -136,6 +129,14 @@
                 dev = (y * 2 + core, j * NZ + z)
                 send(sp.at[over + core, pl.ds(j * SB, SB)], frecv.at[row], f1s.at[core * NY + j], f1r.at[row], dev)
                 send(su.at[over + core], furecv.at[row], fu1s.at[core * NY + j], fu1r.at[row], dev)
+    for i in range(1, ROWS):
+        peer = lax.rem(row + i, ROWS)
+
+        @pl.when(peer // 2 != lax.rem(y + 2, NY))
+        def _():
+            send(sp.at[peer], srecv.at[row], s1s.at[i], s1r.at[i], (peer, col))
+            send(su.at[peer], urecv.at[row], u1s.at[i], u1r.at[i], (peer, col))
+
     for load in loads:
         load.start()
 

time: 51.1 us -> 51.1 us (level)
  no operation moved by 1% of the time
where the time goes in v5:
time: 51.1 us; the launch traced here: 51 us
  Pallas kernels  50.3 us (98%)
  between operations  0.64 us (1%)
    pallas_call x1, Pallas kernels, per_device(): pl.pallas_call(exchange, out_shape=(jax.ShapeDtypeStruct((FB, R), f32), j...  46.7 us
    pallas_call x1, Pallas kernels, per_device(): pl.pallas_call(finish, out_shape=(jax.ShapeDtypeStruct((FB, DB), f32), ja...  3.63 us

profile of v5, /device:TPU:1, one launch (start us, length us, event | category | flops | bytes accessed | tf_op | source)
XLA Modules:
  0.0 51.0 jit_solution(2302092295653090472)
XLA Ops:
  0.6 46.7 %shard_map.76 = (f32[688,512]{1,0:T(8,128)S(1)}, f32[1,512]{1,0:T(1,128)S(1)}, f32[64]{0:T(128)S(1)}, f32[688]{0:T(1024)S(1)}, f32[688,128]{1,0:T(8,128)S(1)}, /...) custom-call(bf16[128,1024]{1,0:T(8,128)(2,1)} %act.1, bf16[688,512]{1,0:T(8,128)(2,1)} %bitcast.2, ...), custom_call_target="tpu_custom_call" | custom-call | tf_op jit(solution)/shard_map/pallas_call | solution.py:476
  47.3 3.6 %shard_map.77 = (f32[688,1024]{1,0:T(8,128)}, f32[64]{0:T(128)}, f32[688]{0:T(1024)}) custom-call(f32[688,512]{1,0:T(8,128)S(1)} %get-tuple-element.13.u, f32[1,512]{1,0:T(1,128)S(1)} %get-tuple-element.14.rows, f32[64]{0:T(128)S(1)} %get-tuple-element.15.rn, f32[688]{0:T(1024)S(1)} %get-tuple-element.16.cn, f32[688,128]{1,0:T(8,128)S(1)} %get-tuple-element.17.by_col, ...), custom_call_target="tpu_custom_call" | custom-call | tf_op jit(solution)/shard_map/pallas_call | solution.py:537
